TPU v7x, 128 devices: a whole 4x4x4 slice. The times are simulated.
128 devices in a mesh: pool: 4 (over x_lo, core), dev: 32 (over x_hi, y, z).
Axes of the slice: x: 4 (x_hi: 2, x_lo: 2; x = x_hi * 2 + x_lo), y: 4, z: 4, core: 2. Of those that a mesh axis runs over, the one named last changes fastest.
Arguments:
- query: bfloat16 [512, 3072], P(('pool', 'dev')), may hold values from -90 to 90
- new_key: bfloat16 [512, 512], P(('pool', 'dev')), may hold values from -4 to 4
- new_value: bfloat16 [512, 512], P(('pool', 'dev')), may hold values from -6 to 6
- key_cache: bfloat16 [512, 512, 512], P(('pool', 'dev')), may hold values from -3 to 3
- value_cache: bfloat16 [512, 512, 512], P(('pool', 'dev')), may hold values from -6 to 6
- lengths: int32 [512], P(('pool', 'dev')), may hold values from 64 to 512, as said below
- hidden_in: bfloat16 [512, 6144], P('pool', 'dev'), may hold values from -6 to 6
- w_out: bfloat16 [3072, 6144], P(None, 'dev'), may hold values from -0.5 to 0.5
- expert_ids: int32 [512, 2], P('pool'), may hold values from 0 to 7, all different within a row; in each aligned block of 128 rows (0 to 127, 128 to 255, ...) at most 80 rows name the same one
- gate_weights: float32 [512, 2], P('pool'), may hold values from 0.2 to 1
- w_gate: bfloat16 [8, 6144, 8192], P('pool', None, 'dev'), may hold values from -0.078125 to 0.078125
- w_up: bfloat16 [8, 6144, 8192], P('pool', None, 'dev'), may hold values from -0.078125 to 0.078125
- w_down: bfloat16 [8, 8192, 6144], P('pool', 'dev'), may hold values from -0.125 to 0.125
Outputs:
- mixed: bfloat16 [512, 6144], P('pool', 'dev')
Inputs may be any that keep to these rules, and one draw needn't show every extreme that they name: `expert_ids`: every row names 2 different experts; among the rows of one micro-batch (aligned blocks of 128 rows) no expert is named by more than 80 rows, a bound that some block reaches. `lengths`: some row has all 512 positions in use.
All inputs are finite; a program needn't handle non-finite values.
Results may differ from a plain program's by a relative error of at most 0.011.
Values may be sent and summed in bfloat16 or wider, within the bound.
A program may use at most 192 MiB of HBM per device.

v0:
```python
import jax
import jax.numpy as jnp
from jax import lax
from jax.sharding import PartitionSpec as P

EXPERTS = 8
HEADS = 24
KV_HEADS = 4
HEAD_DIM = 128


floor_value = -1e30


def shards(
    query,
    new_key,
    new_value,
    key_cache,
    value_cache,
    lengths,
    hidden_in,
    w_out,
    expert_ids,
    gate_weights,
    w_gate,
    w_up,
    w_down,
):
    local_rows = query.shape[0]
    context = key_cache.shape[1]
    group_size = HEADS // KV_HEADS
    score_scale = HEAD_DIM ** (-0.5)
    queries = query.reshape(local_rows, KV_HEADS, group_size, HEAD_DIM)
    cached_keys = key_cache.reshape(local_rows, context, KV_HEADS, HEAD_DIM)
    cached_values = value_cache.reshape(local_rows, context, KV_HEADS, HEAD_DIM)
    scores = (
        jnp.einsum("rkgd,rtkd->rkgt", queries, cached_keys, preferred_element_type=jnp.float32)
        * score_scale
    )
    usable = (jnp.arange(context)[None, :] < lengths[:, None])[:, None, None, :]
    row_max = jnp.max(jnp.where(usable, scores, floor_value), axis=-1)
    weights = jnp.where(usable, jnp.exp(scores - row_max[..., None]), 0.0)
    weight_total = jnp.sum(weights, axis=-1)
    cache_sum = jnp.einsum(
        "rkgt,rtkd->rkgd",
        weights.astype(jnp.bfloat16),
        cached_values,
        preferred_element_type=jnp.float32,
    )
    fresh_keys = new_key.reshape(local_rows, KV_HEADS, HEAD_DIM)
    fresh_score = (
        jnp.einsum("rkgd,rkd->rkg", queries, fresh_keys, preferred_element_type=jnp.float32)
        * score_scale
    )
    final_max = jnp.maximum(row_max, fresh_score)
    cache_factor = jnp.exp(row_max - final_max)
    fresh_factor = jnp.exp(fresh_score - final_max)
    fresh_values = new_value.reshape(local_rows, KV_HEADS, 1, HEAD_DIM).astype(jnp.float32)
    numerator = cache_sum * cache_factor[..., None] + fresh_factor[..., None] * fresh_values
    attended = numerator / (weight_total * cache_factor + fresh_factor)[..., None]
    attended = attended.astype(jnp.bfloat16).reshape(local_rows, HEADS * HEAD_DIM)
    projected = jnp.dot(
        lax.all_gather(attended, "dev", axis=0, tiled=True),
        w_out,
        preferred_element_type=jnp.float32,
    )
    middle = (hidden_in.astype(jnp.float32) + projected).astype(jnp.bfloat16)
    group_rows = middle.shape[0]
    capacity = group_rows * 5 // 8
    pool_count = lax.axis_size("pool")
    local_experts = w_gate.shape[0]
    picked = expert_ids[:, :, None] == jnp.arange(EXPERTS)[None, None, :]
    routed = jnp.any(picked, axis=1)
    route_weight = jnp.sum(jnp.where(picked, gate_weights[:, :, None], 0.0), axis=1)
    routed_int = routed.astype(jnp.int32)
    earlier = jnp.cumsum(routed_int, axis=0) - routed_int
    placed = routed[:, :, None] & (earlier[:, :, None] == jnp.arange(capacity)[None, None, :])
    dispatch_table = placed.astype(jnp.bfloat16)
    combine_table = jnp.where(placed, route_weight[:, :, None], 0.0)
    features = lax.all_gather(middle, "dev", axis=1, tiled=True)
    outgoing = jnp.einsum(
        "rec,rd->ecd", dispatch_table, features, preferred_element_type=jnp.float32
    ).astype(jnp.bfloat16)
    outgoing = outgoing.reshape(pool_count, local_experts, capacity, features.shape[1])
    arrived = lax.all_to_all(outgoing, "pool", split_axis=0, concat_axis=0, tiled=True)
    gate_part = jnp.einsum("secd,edf->secf", arrived, w_gate, preferred_element_type=jnp.float32)
    up_part = jnp.einsum("secd,edf->secf", arrived, w_up, preferred_element_type=jnp.float32)
    hidden_units = (jax.nn.silu(gate_part) * up_part).astype(jnp.bfloat16)
    partial_value = jnp.einsum(
        "secf,efd->secd", hidden_units, w_down, preferred_element_type=jnp.float32
    )
    owned_sums = lax.psum_scatter(partial_value, "dev", scatter_dimension=3, tiled=True)
    returned = lax.all_to_all(owned_sums, "pool", split_axis=0, concat_axis=0, tiled=True)
    returned = returned.reshape(EXPERTS, capacity, owned_sums.shape[3])
    mixture = jnp.einsum("rec,ecd->rd", combine_table, returned, precision=lax.Precision.HIGHEST)
    return (middle.astype(jnp.float32) + mixture).astype(jnp.bfloat16)


def solution(mesh):
    return jax.shard_map(
        shards,
        mesh=mesh,
        in_specs=(
            P(("pool", "dev"), None),
            P(("pool", "dev"), None),
            P(("pool", "dev"), None),
            P(("pool", "dev"), None, None),
            P(("pool", "dev"), None, None),
            P(("pool", "dev")),
            P("pool", "dev"),
            P(None, "dev"),
            P("pool", None),
            P("pool", None),
            P("pool", None, "dev"),
            P("pool", None, "dev"),
            P("pool", "dev", None),
        ),
        out_specs=P("pool", "dev"),
        check_vma=False,
    )
```

profile of v0, /device:TPU:0, one launch (start us, length us, event | category | flops | bytes accessed | tf_op | source)
XLA Modules:
  0.0 627.2 jit_solution(14822471497189863600)
XLA Ops:
  6.6 0.9 iota_compare_fusion.2
  7.5 0.9 reshape.68
  8.3 0.7 reshape.87
  9.0 0.7 reshape.75
  9.9 0.7 select_reduce_fusion
  10.6 0.2 fusion.56
  10.9 2.0 fusion.49
  12.9 100.7 %all-gather = bf16[32,4,3072]{2,1,0:T(4,128)(2,1)S(1)} all-gather(bf16[1,4,3072]{2,1,0:T(4,128)(2,1)S(1)} %reshape.76), channel_id=1, replica_groups=mesh['pool'=4,'dev'=32] {'dev'}, dimensions={0}, use_global_device_ids=true | all-gather | bytes 811008 | tf_op jit(solution)/shard_map/all_gather | solution.py:64
  113.7 0.2 reshape.77
  113.9 1.1 fusion.39
  115.4 62.7 %all-gather.3.cloned.1.call-done = bf16[128,6144]{0,1:T(8,128)(2,1)} async-done(((bf16[128,192]{0,1:T(8,128)(2,1)}), bf16[128,6144]{0,1:T(8,128)(2,1)}) %all-gather.3.cloned.1.call-update) | async-done | bytes 1572880 | tf_op jit(solution)/shard_map/all_gather | solution.py:81
  178.1 3.6 convolution_convert_fusion
  181.7 90.2 %all_to_all.10 = bf16[4,2,80,6144]{3,2,1,0:T(8,128)(2,1)S(1)} all-to-all(bf16[4,2,80,6144]{3,2,1,0:T(8,128)(2,1)S(1)} %bitcast.83), channel_id=1, replica_groups=mesh['pool'=4,'dev'=32] {'pool'}, dimensions={0} | all-to-all | bytes 15728640 | tf_op jit(solution)/shard_map/all_to_all | solution.py:86
  272.0 5.1 fusion.14
  277.1 5.2 fusion.29
  282.3 7.7 %convolution_bitcast_fusion = f32[4,2,80,6144]{3,2,0,1:T(8,128)} fusion(bf16[4,2,80,256]{3,2,0,1:T(8,128)(2,1)S(1)} %fusion.29, bf16[2,256,6144]{2,1,0:T(8,128)(2,1)S(1)} %bitcast.85), kind=kOutput, calls=%fused_computation | convolution fusion | flops 2013265920 | bytes 22347776 | tf_op jit(solution)/shard_map/secf,efd->secd/dot_general | solution.py:90
  289.9 23.9 %copy.51 = f32[4,2,80,6144]{2,0,1,3:T(4,128)} copy(f32[4,2,80,6144]{3,2,0,1:T(8,128)} %convolution_bitcast_fusion) | data formatting | bytes 31457280
  313.9 26.8 %reshape.88 = f32[6144,640]{1,0:T(8,128)} reshape(f32[6144,2,4,80]{3,2,1,0:T(4,128)} %bitcast.82) | data formatting | bytes 31457280
  340.7 261.1 %reduce-scatter.4.cloned.1.call-done = f32[192,640]{1,0:T(8,128)} async-done(((f32[6144,640]{1,0:T(8,128)}), f32[192,640]{1,0:T(8,128)}) %reduce-scatter.4.cloned.1.call-update) | async-done | bytes 491536
  601.8 1.8 reshape.89
  603.6 1.3 copy.45
  604.9 3.5 all-to-all-start.1
  608.4 10.2 %all-to-all-done.1 = f32[4,2,80,192]{3,2,1,0:T(8,128)S(1)} async-done(((f32[4,2,80,192]{3,2,1,0:T(8,128)}), f32[4,2,80,192]{3,2,1,0:T(8,128)S(1)}, u32[]{:S(2)}, u32[]{:S(2)}) %all-to-all-start.1) | async-done | bytes 491552 | tf_op jit(solution)/shard_map/all_to_all | solution.py:94
  618.6 1.8 fusion.38
  (33 shorter events, 0.7 us)
Async XLA Ops:
  6.5 3.3 copy-start
  6.5 107.3 %copy-start.4 = (bf16[128,192]{0,1:T(8,128)(2,1)S(1)}, bf16[128,192]{0,1:T(8,128)(2,1)}, u32[]{:S(2)}) copy-start(bf16[128,192]{0,1:T(8,128)(2,1)} %param.19) | copy-start | bytes 147460
  6.5 107.3 %copy-start.2 = (bf16[3072,192]{0,1:T(8,128)(2,1)S(1)}, bf16[3072,192]{0,1:T(8,128)(2,1)}, u32[]{:S(2)}) copy-start(bf16[3072,192]{0,1:T(8,128)(2,1)} %param.20) | copy-start | bytes 3538948
  6.5 108.5 %copy-start.5 = (s32[128,2]{0,1:T(2,128)S(1)}, s32[128,2]{0,1:T(2,128)}, u32[]{:S(2)}) copy-start(s32[128,2]{0,1:T(2,128)} %param.21) | copy-start | bytes 3076
  6.5 171.6 %all-gather.3.cloned.1.call-start = ((), (), s32[]{:S(2)}) async-start(), calls=%async_computation.3 | async-start | bytes 1622016 | tf_op jit(solution)/shard_map/all_gather | solution.py:81
  115.0 486.8 %reduce-scatter.4.cloned.1.call-start = ((), (), s32[]{:S(2)}) async-start(), calls=%async_computation.4 | async-start | bytes 16220160
  272.0 10.3 %slice-start = ((s8[6291456]{0:T(1024)(128)(4,1)}), s8[4194304]{0:T(1024)(128)(4,1)S(1)}, s32[]{:S(2)}) async-start(s8[6291456]{0:T(1024)(128)(4,1)} %bitcast.84), calls=%async_computation.5 | async-start | bytes 8388608
  277.1 5.2 slice-start.1
  340.6 267.7 %copy-start.6 = (f32[128,2]{0,1:T(2,128)S(1)}, f32[128,2]{0,1:T(2,128)}, u32[]{:S(2)}) copy-start(f32[128,2]{0,1:T(2,128)} %param.22) | copy-start | bytes 3076
  340.6 277.9 %copy-start.3 = (bf16[128,192]{0,1:T(8,128)(2,1)S(1)}, bf16[128,192]{0,1:T(8,128)(2,1)}, u32[]{:S(2)}) copy-start(bf16[128,192]{0,1:T(8,128)(2,1)} %fusion.39) | copy-start | bytes 147460
  340.7 279.7 %copy-start.1 = (bf16[4,512,512]{2,1,0:T(8,128)(2,1)S(1)}, bf16[4,512,512]{2,1,0:T(8,128)(2,1)}, u32[]{:S(2)}) copy-start(bf16[4,512,512]{2,1,0:T(8,128)(2,1)} %param.16) | copy-start | bytes 6291460
  604.9 13.7 %all-to-all-start.1 = ((f32[4,2,80,192]{3,2,1,0:T(8,128)}), f32[4,2,80,192]{3,2,1,0:T(8,128)S(1)}, u32[]{:S(2)}, u32[]{:S(2)}) async-start(f32[4,2,80,192]{3,2,1,0:T(8,128)} %copy.45), calls=%async_computation.1 | async-start | bytes 1310720 | tf_op jit(solution)/shard_map/all_to_all | solution.py:94
Sparse Core Ops, SparseCore 0:
  115.1 62.9 all-gather.2
  340.8 260.9 reduce-scatter.3
where the time goes:
time: 629 us; the launch traced here: 627 us
  waiting for transfers between devices  334 us (53%)
  blocking collectives  191 us (30%)
  local copies, waits for them, and re-layouts  56.4 us (9%)
  matrix products  27.4 us (4%)
  between operations  13.6 us (2%)
    unnamed x3, waiting for transfers between devices  261 us
    all_gather x1, blocking collectives, shards(): lax.all_gather(attended, 'dev', axis=0, tiled=True)  101 us
    all_to_all x1, blocking collectives, shards(): lax.all_to_all(outgoing, 'pool', split_axis=0, concat_axis=0, tiled=True)  90.2 us
    all_gather x1, waiting for transfers between devices, shards(): features = lax.all_gather(middle, 'dev', axis=1, tiled=True)  62.7 us
    unnamed x23, local copies, waits for them, and re-layouts  52.7 us
  transfers between devices with their start and end apart: 3, of which 3 were waited for; matrix products, arithmetic and copies ran while one was open for 0% of the time, Pallas kernels for 0%

commit v1 on v0

v1 whole, which is shorter than its diff:
```python
import jax
import jax.numpy as jnp
from jax import lax
from jax.experimental import pallas as pl
from jax.experimental.pallas import tpu as pltpu
from jax.sharding import PartitionSpec as P

EXPERTS = 8
HEADS = 24
KV_HEADS = 4
HEAD_DIM = 128
WIDTH = 6144
UNITS = 256

MESH = pl.DeviceIdType.MESH
floor_value = -1e30

GATHER_ORDER = ("zyx", "yxz", "xzy")
REDUCE_ORDER = ("xyz", "zxy", "yzx")


def layer_kernel(
    att_ref, ids_ref, weight_ref, hidden_ref, wout_ref, wg_hbm, wu_hbm, wd_hbm,
    out_ref,
    wcat, wd, at, g, route, s_mine, s_sib, from_sib, ring1, ring2, ring3, acc, hs_mine, hs_sib, mid, fin,
    lsem, ssem, rsem,
):
    f32, bf16 = jnp.float32, jnp.bfloat16
    pool, dev = lax.axis_index("pool"), lax.axis_index("dev")
    xl, c = pool // 2, pool % 2
    xh, y, z = dev // 16, (dev // 4) % 4, dev % 4
    x = 2 * xh + xl
    odd = (z % 2) == 1
    where_at = {"x": x, "y": y, "z": z}

    def ident(x_, y_, z_, c_):
        return ((x_ % 2) * 2 + c_, (x_ // 2) * 16 + y_ * 4 + z_)

    def near(axis, step):
        p = dict(where_at)
        p[axis] = (p[axis] + step + 4) % 4
        return ident(p["x"], p["y"], p["z"], c)

    sibling = ident(x, y, z, 1 - c)
    opposite = ident((x + 2) % 4, y, z, c)
    beside = x + 1 - 2 * xl
    beside_same = ident(beside, y, z, c)
    beside_other = ident(beside, y, z, 1 - c)

    local = []
    for e in range(2):
        for half in range(2):
            rows = pl.ds(half * (WIDTH // 2), WIDTH // 2)
            local.append(pltpu.make_async_copy(
                wg_hbm.at[e, rows], wcat.at[rows, pl.ds(e * 512, UNITS)], lsem.at[len(local)]))
            local.append(pltpu.make_async_copy(
                wu_hbm.at[e, rows], wcat.at[rows, pl.ds(e * 512 + UNITS, UNITS)], lsem.at[len(local)]))
    n_up = len(local)
    for e in range(2):
        local.append(pltpu.make_async_copy(wd_hbm.at[e], wd.at[pl.ds(e * UNITS, UNITS)], lsem.at[len(local)]))
    for cp in local:
        cp.start()

    barrier = pltpu.get_barrier_semaphore()
    greeted = [near(a, d) for a in "xyz" for d in (1, -1)] + [sibling, opposite, beside_other]
    for who in greeted:
        pl.semaphore_signal(barrier, inc=1, device_id=who, device_id_type=MESH)

    at[0, xh, y, z] = att_ref[0:48]
    at[1, xh, y, z] = att_ref[48:96]
    lane = lax.broadcasted_iota(jnp.int32, (128, 128), 1)
    table = jnp.zeros((128, 128), f32)
    for k in range(2):
        table = table + jnp.where(ids_ref[:, k:k + 1] == lane, weight_ref[:, k:k + 1], 0.0)
    route[c, xl] = table
    pl.semaphore_wait(barrier, len(greeted))

    used = [0]
    sent = []

    def send(src, dst, who):
        k = used[0]
        used[0] += 1
        cp = pltpu.make_async_remote_copy(
            src_ref=src, dst_ref=dst, send_sem=ssem.at[k], recv_sem=rsem.at[k],
            device_id=who, device_id_type=MESH)
        cp.start()
        sent.append(cp)
        return cp

    cross = send(at.at[:, xh, y, z], at.at[:, xh, y, z], opposite)
    route_copies = [send(route.at[c, xl], route.at[c, xl], who) for who in (sibling, beside_same, beside_other)]

    def at_chunk(q, stage, i, half=None):
        xs = slice(None) if half is None else half
        if stage == 0:
            return at.at[q, xs, y, i] if q == 0 else at.at[q, xs, i, z]
        return at.at[q, xs, i] if q == 0 else at.at[q, xs, :, i]

    def ring_gather(parts):
        ahead, back, ends = [], [], []
        for axis, chunk in parts:
            i = where_at[axis]
            ahead.append(send(chunk(i), chunk(i), near(axis, 1)))
            back.append(send(chunk(i), chunk(i), near(axis, -1)))
        for n, (axis, chunk) in enumerate(parts):
            i = where_at[axis]
            before, after = (i + 3) % 4, (i + 1) % 4
            ahead[n].wait_recv()
            one = send(chunk(before, 0), chunk(before, 0), near(axis, 1))
            back[n].wait_recv()
            two = send(chunk(after, 1), chunk(after, 1), near(axis, -1))
            ends.append((one, two))
        for one, two in ends:
            one.wait_recv()
            two.wait_recv()

    cross.wait_recv()
    for stage in range(2):
        axes = ("z", "y") if stage == 0 else ("y", "z")
        ring_gather([
            (axes[q], lambda i, half=None, q=q, stage=stage: at_chunk(q, stage, i, half)) for q in range(2)])

    total = jnp.zeros((128, 192), f32)
    low = (lax.broadcasted_iota(jnp.int32, (16, 48, 128), 1) % 8) < 4
    for q in range(2):
        rows = at[q].astype(f32).reshape(16, 2, 48, 128)
        a, b = rows[:, 0], rows[:, 1]
        even = jnp.where(low, a, pltpu.roll(b, 4, 1)).reshape(16, 6, 8, 128)
        unev = jnp.where(low, pltpu.roll(a, 44, 1), b).reshape(16, 6, 8, 128)
        heads = []
        for v in range(6):
            heads.append(even[:, v].reshape(128, 128).astype(bf16))
            heads.append(unev[:, v].reshape(128, 128).astype(bf16))
        total = total + jnp.dot(
            jnp.concatenate(heads, axis=1), wout_ref[q * 1536:(q + 1) * 1536, :], preferred_element_type=f32)
    middle = (hidden_ref[...].astype(f32) + total).astype(bf16).astype(f32)
    mid[:, 128:256] = jnp.zeros((128, 128), f32)
    mid[:, 0:192] = middle

    lane64 = lax.broadcasted_iota(jnp.int32, (64, 128), 1) < 64
    lane128 = lane < 64
    t0, t1 = mid[:, 0:128], mid[:, 128:256]
    whole = jnp.where(odd, jnp.where(lane128, pltpu.roll(t0, 64, 1), pltpu.roll(t1, 64, 1)), t0)
    packed = jnp.where(
        odd,
        jnp.where(lane64, t0[64:128], pltpu.roll(t0[0:64], 64, 1)),
        jnp.where(lane64, t1[0:64], pltpu.roll(t1[64:128], 64, 1)),
    )
    g[0, c, x, y, z] = whole[0:64].astype(bf16)
    g[1, c, x, y, z] = whole[64:128].astype(bf16)
    g[2, c, x, y, z] = packed.astype(bf16)

    def view(ref, lead, order, stage, i, half=None):
        where = []
        for axis in "xyz":
            at_stage = order.index(axis)
            where.append(i if at_stage == stage else slice(None) if at_stage < stage else where_at[axis])
        rows = slice(None) if half is None else pl.ds(half * 32, 32)
        return ref.at[(*lead, *where, rows)]

    passed = []

    def hand_over(q, stage, i):
        v = view(g, (q, c), GATHER_ORDER[q], stage, i)
        passed.append(send(v, v, sibling))

    for stage in range(3):
        parts = [
            (GATHER_ORDER[q][stage],
             lambda i, half=None, q=q, stage=stage: view(g, (q, c), GATHER_ORDER[q], stage, i, half))
            for q in range(3)
        ]
        if stage < 2:
            ring_gather(parts)
            continue
        ahead, back, ends = [], [], []
        for axis, chunk in parts:
            i = where_at[axis]
            ahead.append(send(chunk(i), chunk(i), near(axis, 1)))
            back.append(send(chunk(i), chunk(i), near(axis, -1)))
        for q in range(3):
            hand_over(q, 2, where_at[parts[q][0]])
        for q, (axis, chunk) in enumerate(parts):
            i = where_at[axis]
            before, after = (i + 3) % 4, (i + 1) % 4
            ahead[q].wait_recv()
            one = send(chunk(before, 0), chunk(before, 0), near(axis, 1))
            back[q].wait_recv()
            two = send(chunk(after, 1), chunk(after, 1), near(axis, -1))
            ends.append((one, two))
            hand_over(q, 2, before)
            hand_over(q, 2, after)
        for q, (one, two) in enumerate(ends):
            one.wait_recv()
            two.wait_recv()
            hand_over(q, 2, (where_at[parts[q][0]] + 2) % 4)

    for cp in local[:n_up]:
        cp.wait()

    lane2 = lax.broadcasted_iota(jnp.int32, (2, 64, 128), 2) < 64

    def gate_and_up(plane, hs):
        acc[...] = jnp.zeros((256, 1024), f32)

        @pl.loop(0, 8)
        def _(i):
            xi, yi = i // 4, i % 4
            tiles = []
            for zp in range(2):
                pieces = []
                for zz in range(2):
                    a = g[0:2, plane, pl.ds(2 * xi, 2), yi, 2 * zp + zz]
                    pieces.append(a.reshape(256, 128))
                h0 = g[2, plane, pl.ds(2 * xi, 2), yi, 2 * zp].astype(f32)
                h1 = g[2, plane, pl.ds(2 * xi, 2), yi, 2 * zp + 1].astype(f32)
                upper = jnp.where(lane2, h0, h1).reshape(128, 128)
                lower = pltpu.roll(jnp.where(lane2, h1, h0).reshape(128, 128), 64, 1)
                halves = jnp.concatenate([upper, lower], axis=0).astype(bf16)
                tiles += [pieces[0], halves, pieces[1]]
            lhs = jnp.concatenate(tiles, axis=1)
            rhs = wcat[pl.ds(pl.multiple_of(i * 768, 768), 768), :]
            acc[...] += jnp.dot(lhs, rhs, preferred_element_type=f32)

        lanes = lax.broadcasted_iota(jnp.int32, (64, 128), 1)
        for e in range(2):
            cols = []
            for half in range(2):
                for xi in range(2):
                    t = route[plane, xi, half * 64:(half + 1) * 64, :]
                    cols.append(jnp.sum(jnp.where(lanes == 2 * pool + e, t, 0.0), axis=1, keepdims=True))
            col = jnp.concatenate(cols, axis=0)
            gate = acc[:, e * 512:e * 512 + 256]
            up = acc[:, e * 512 + 256:e * 512 + 512]
            hs[:, e * 256:(e + 1) * 256] = (gate / (1.0 + jnp.exp(-gate)) * up * col).astype(bf16)

    def down(hs, i):
        return jnp.dot(
            hs[...], wd[:, pl.ds(pl.multiple_of(i * 768, 768), 768)], preferred_element_type=f32)

    def parts_of(out):
        got = []
        for zp in range(2):
            tiles = [out[:, zp * 384 + k * 128:zp * 384 + (k + 1) * 128] for k in range(3)]
            upper = tiles[1][0:128].reshape(2, 64, 128)
            lower = pltpu.roll(tiles[1][128:256], 64, 1).reshape(2, 64, 128)
            got.append((tiles[0].reshape(2, 2, 64, 128), jnp.where(lane2, upper, lower)))
            got.append((tiles[2].reshape(2, 2, 64, 128), jnp.where(lane2, lower, upper)))
        return got

    for cp in route_copies:
        cp.wait_recv()

    gate_and_up(c, hs_mine)
    for cp in passed:
        cp.wait_recv()
    gate_and_up(1 - c, hs_sib)
    for cp in local[n_up:]:
        cp.wait()

    base = used[0]
    used[0] += 8

    def sib_copy(i):
        part = (slice(None), pl.ds(2 * (i // 4), 2), i % 4)
        return pltpu.make_async_remote_copy(
            src_ref=s_sib.at[part], dst_ref=from_sib.at[part], send_sem=ssem.at[base + i],
            recv_sem=rsem.at[base + i], device_id=sibling, device_id_type=MESH)

    @pl.loop(0, 8)
    def _(i):
        xi, yi = i // 4, i % 4
        for zi, (a, h) in enumerate(parts_of(down(hs_sib, i))):
            s_sib[0:2, pl.ds(2 * xi, 2), yi, zi] = a.astype(bf16)
            s_sib[2, pl.ds(2 * xi, 2), yi, zi] = h.astype(bf16)
        sib_copy(i).start()

    @pl.loop(0, 8)
    def _(i):
        xi, yi = i // 4, i % 4
        sib_copy(i).wait_recv()
        for zi, (a, h) in enumerate(parts_of(down(hs_mine, i))):
            fa = from_sib[0:2, pl.ds(2 * xi, 2), yi, zi].astype(f32)
            fh = from_sib[2, pl.ds(2 * xi, 2), yi, zi].astype(f32)
            s_mine[0:2, pl.ds(2 * xi, 2), yi, zi] = (a + fa).astype(bf16)
            s_mine[2, pl.ds(2 * xi, 2), yi, zi] = (h + fh).astype(bf16)

    def chunk_of(q, stage, i, half):
        order = REDUCE_ORDER[q]
        where = []
        for axis in "xyz":
            at_stage = order.index(axis)
            where.append(i if at_stage == stage else slice(None) if at_stage > stage else where_at[axis])
        return s_mine.at[(q, *where, pl.ds(half * 32, 32))]

    for stage, ring in enumerate((ring1, ring2, ring3)):
        firsts, seconds, thirds = [], [], []
        for q in range(3):
            axis = REDUCE_ORDER[q][stage]
            i = where_at[axis]
            before, after, far = (i + 3) % 4, (i + 1) % 4, (i + 2) % 4
            firsts.append((
                send(chunk_of(q, stage, far, 0), ring.at[q, 0], near(axis, 1)),
                send(chunk_of(q, stage, far, 1), ring.at[q, 1], near(axis, -1))))
            seconds.append((
                send(chunk_of(q, stage, after, 1), ring.at[q, 2], near(axis, 1)),
                send(chunk_of(q, stage, before, 0), ring.at[q, 3], near(axis, -1))))
        for q in range(3):
            axis = REDUCE_ORDER[q][stage]
            i = where_at[axis]
            before, after = (i + 3) % 4, (i + 1) % 4
            ahead, back = firsts[q]
            ahead.wait_recv()
            v = chunk_of(q, stage, after, 0)
            v[...] = (v[...].astype(f32) + ring[q, 0].astype(f32)).astype(bf16)
            one = send(v, ring.at[q, 4], near(axis, 1))
            back.wait_recv()
            v = chunk_of(q, stage, before, 1)
            v[...] = (v[...].astype(f32) + ring[q, 1].astype(f32)).astype(bf16)
            two = send(v, ring.at[q, 5], near(axis, -1))
            thirds.append((one, two))
        for q in range(3):
            i = where_at[REDUCE_ORDER[q][stage]]
            for cp in seconds[q] + thirds[q]:
                cp.wait_recv()
            first = (chunk_of(q, stage, i, 0)[...].astype(f32)
                     + ring[q, 4].astype(f32) + ring[q, 3].astype(f32))
            second = (chunk_of(q, stage, i, 1)[...].astype(f32)
                      + ring[q, 2].astype(f32) + ring[q, 5].astype(f32))
            if stage < 2:
                chunk_of(q, stage, i, 0)[...] = first.astype(bf16)
                chunk_of(q, stage, i, 1)[...] = second.astype(bf16)
            else:
                fin[q, 0:32] = first
                fin[q, 32:64] = second

    whole = fin[0:2].reshape(128, 128)
    rolled = pltpu.roll(whole, 64, 1)
    f2 = fin[2]
    r2 = pltpu.roll(f2, 64, 1)
    left = jnp.where(odd, jnp.where(lane128, jnp.concatenate([r2, f2], axis=0), rolled), whole)
    right = jnp.where(odd, rolled, jnp.concatenate([f2, r2], axis=0))
    mid[:, 0:128] += left
    mid[:, 128:256] += right
    out_ref[...] = mid[:, 0:192].astype(bf16)

    for cp in sent:
        cp.wait_send()

    @pl.loop(0, 8)
    def _(i):
        sib_copy(i).wait_send()


def attention(query, new_key, new_value, key_cache, value_cache, lengths):
    local_rows = query.shape[0]
    context = key_cache.shape[1]
    group_size = HEADS // KV_HEADS
    score_scale = HEAD_DIM ** (-0.5)
    queries = query.reshape(local_rows, KV_HEADS, group_size, HEAD_DIM)
    cached_keys = key_cache.reshape(local_rows, context, KV_HEADS, HEAD_DIM)
    cached_values = value_cache.reshape(local_rows, context, KV_HEADS, HEAD_DIM)
    scores = (
        jnp.einsum("rkgd,rtkd->rkgt", queries, cached_keys, preferred_element_type=jnp.float32)
        * score_scale
    )
    usable = (jnp.arange(context)[None, :] < lengths[:, None])[:, None, None, :]
    row_max = jnp.max(jnp.where(usable, scores, floor_value), axis=-1)
    weights = jnp.where(usable, jnp.exp(scores - row_max[..., None]), 0.0)
    weight_total = jnp.sum(weights, axis=-1)
    cache_sum = jnp.einsum(
        "rkgt,rtkd->rkgd",
        weights.astype(jnp.bfloat16),
        cached_values,
        preferred_element_type=jnp.float32,
    )
    fresh_keys = new_key.reshape(local_rows, KV_HEADS, HEAD_DIM)
    fresh_score = (
        jnp.einsum("rkgd,rkd->rkg", queries, fresh_keys, preferred_element_type=jnp.float32)
        * score_scale
    )
    final_max = jnp.maximum(row_max, fresh_score)
    cache_factor = jnp.exp(row_max - final_max)
    fresh_factor = jnp.exp(fresh_score - final_max)
    fresh_values = new_value.reshape(local_rows, KV_HEADS, 1, HEAD_DIM).astype(jnp.float32)
    numerator = cache_sum * cache_factor[..., None] + fresh_factor[..., None] * fresh_values
    attended = numerator / (weight_total * cache_factor + fresh_factor)[..., None]
    return attended.astype(jnp.bfloat16)


def shards(
    query,
    new_key,
    new_value,
    key_cache,
    value_cache,
    lengths,
    hidden_in,
    w_out,
    expert_ids,
    gate_weights,
    w_gate,
    w_up,
    w_down,
):
    attended = attention(query, new_key, new_value, key_cache, value_cache, lengths)
    attended = attended.reshape(4, HEADS, HEAD_DIM).transpose(1, 0, 2).reshape(96, HEAD_DIM)
    bf16, f32 = jnp.bfloat16, jnp.float32
    vmem = pl.BlockSpec(memory_space=pltpu.VMEM)
    hbm = pl.BlockSpec(memory_space=pl.ANY)
    return pl.pallas_call(
        layer_kernel,
        out_shape=jax.ShapeDtypeStruct((128, 192), bf16),
        in_specs=[vmem] * 5 + [hbm] * 3,
        out_specs=vmem,
        scratch_shapes=[
            pltpu.VMEM((WIDTH, 4 * UNITS), bf16),
            pltpu.VMEM((2 * UNITS, WIDTH), bf16),
            pltpu.VMEM((2, 2, 4, 4, 48, 128), bf16),
            pltpu.VMEM((3, 2, 4, 4, 4, 64, 128), bf16),
            pltpu.VMEM((2, 2, 128, 128), f32),
            pltpu.VMEM((3, 4, 4, 4, 64, 128), bf16),
            pltpu.VMEM((3, 4, 4, 4, 64, 128), bf16),
            pltpu.VMEM((3, 4, 4, 4, 64, 128), bf16),
            pltpu.VMEM((3, 6, 4, 4, 32, 128), bf16),
            pltpu.VMEM((3, 6, 4, 32, 128), bf16),
            pltpu.VMEM((3, 6, 32, 128), bf16),
            pltpu.VMEM((256, 1024), f32),
            pltpu.VMEM((256, 512), bf16),
            pltpu.VMEM((256, 512), bf16),
            pltpu.VMEM((128, 256), f32),
            pltpu.VMEM((3, 64, 128), f32),
            pltpu.SemaphoreType.DMA((10,)),
            pltpu.SemaphoreType.DMA((144,)),
            pltpu.SemaphoreType.DMA((144,)),
        ],
        compiler_params=pltpu.CompilerParams(
            collective_id=0, has_side_effects=True, vmem_limit_bytes=60 * 1024 * 1024
        ),
        cost_estimate=pl.CostEstimate(flops=10_000_000_000, bytes_accessed=20_000_000, transcendentals=0),
        name="layer",
    )(attended, expert_ids, gate_weights, hidden_in, w_out, w_gate, w_up, w_down)


def solution(mesh):
    return jax.shard_map(
        shards,
        mesh=mesh,
        in_specs=(
            P(("pool", "dev"), None),
            P(("pool", "dev"), None),
            P(("pool", "dev"), None),
            P(("pool", "dev"), None, None),
            P(("pool", "dev"), None, None),
            P(("pool", "dev")),
            P("pool", "dev"),
            P(None, "dev"),
            P("pool", None),
            P("pool", None),
            P("pool", None, "dev"),
            P("pool", None, "dev"),
            P("pool", "dev", None),
        ),
        out_specs=P("pool", "dev"),
        check_vma=False,
    )
```

time: 629 us -> 113 us (0.18)
  waiting for transfers between devices: 334 us -> 0 us
  blocking collectives: 191 us -> 0 us
  Pallas kernels: 0 us -> 98.9 us
  local copies, waits for them, and re-layouts: 56.4 us -> 10.9 us
  matrix products: 27.4 us -> 1.31 us
  between operations: 13.6 us -> 0.03 us
    unnamed x3 -> x0, waiting for transfers between devices: 261 us -> none
    all_gather x1 -> x0, blocking collectives: 101 us -> none  [shards(): lax.all_gather(attended, 'dev', axis=0, tiled=True)]
    pallas_call x0 -> x1, Pallas kernels: none -> 98.9 us  [shards(): pl.pallas_call(layer_kernel, out_shape=jax.ShapeDtypeStruct((128, 192), b...]
    all_to_all x1 -> x0, blocking collectives: 90.2 us -> none  [shards(): lax.all_to_all(outgoing, 'pool', split_axis=0, concat_axis=0, tiled=True)]
    all_gather x1 -> x0, waiting for transfers between devices: 62.7 us -> none  [shards(): features = lax.all_gather(middle, 'dev', axis=1, tiled=True)]
    unnamed x23 -> x10, local copies, waits for them, and re-layouts: 52.7 us -> 6.51 us
    dot_general x9 -> x3, matrix products: 27.4 us -> 1.31 us  [the longest x1 0.73 us: attention(): jnp.einsum('rkgd,rtkd->rkgt', queries, cached_keys, preferred_element_typ...]
    all_to_all x1 -> x0, waiting for transfers between devices: 10.2 us -> none  [shards(): lax.all_to_all(owned_sums, 'pool', split_axis=0, concat_axis=0, tiled=True)]
  transfers between devices with their start and end apart: 3 -> 0, of which waited for: 3 -> 0; matrix products, arithmetic and copies ran while one was open for 0% -> 0% of each run, Pallas kernels for 0% -> 0%
where the time goes in v1:
time: 113 us; the launch traced here: 112 us
  Pallas kernels  98.9 us (88%)
  local copies, waits for them, and re-layouts  10.9 us (10%)
  matrix products  1.31 us (1%)
    pallas_call x1, Pallas kernels, shards(): pl.pallas_call(layer_kernel, out_shape=jax.ShapeDtypeStruct((128, 192), b...  98.9 us
    unnamed x10, local copies, waits for them, and re-layouts  6.51 us

profile of v1, /device:TPU:0, one launch (start us, length us, event | category | flops | bytes accessed | tf_op | source)
XLA Modules:
  0.0 112.3 jit_solution(11394983461413023492)
XLA Ops:
  0.0 0.0 copy-start
  0.0 0.9 iota_compare_fusion
  0.9 0.7 reshape.59
  1.6 0.7 reshape.55
  2.3 0.8 reshape.49
  3.0 0.1 fusion.32
  3.2 1.5 %copy.27.hidden_ref = bf16[128,192]{1,0:T(8,128)(2,1)} copy(bf16[128,192]{0,1:T(8,128)(2,1)} %param.19) | data formatting | bytes 98304 | tf_op args[6]
  4.7 1.4 %copy.25.ids_ref = s32[128,2]{1,0:T(8,128)} copy(s32[128,2]{0,1:T(2,128)} %param.21) | data formatting | bytes 2048 | tf_op args[8]
  6.1 1.4 %copy.26.weight_ref = f32[128,2]{1,0:T(8,128)} copy(f32[128,2]{0,1:T(2,128)} %param.22) | data formatting | bytes 2048 | tf_op args[9]
  7.5 0.0 copy-done
  7.5 0.0 copy-start.2
  7.5 0.7 select_reduce_fusion
  8.2 0.0 copy-start.1
  8.2 0.2 fusion.21
  8.5 0.6 copy-done.2
  9.1 0.4 fusion.18
  9.6 0.6 copy.24
  10.2 0.0 copy-done.1
  10.2 1.6 %copy.28.wout_ref = bf16[3072,192]{1,0:T(8,128)(2,1)} copy(bf16[3072,192]{0,1:T(8,128)(2,1)S(1)} %copy-done.1) | data formatting | bytes 2359296 | tf_op args[7]
  11.7 98.9 %layer.1 = bf16[128,192]{1,0:T(8,128)(2,1)} custom-call(bf16[96,128]{1,0:T(8,128)(2,1)} %bitcast.36, s32[128,2]{1,0:T(8,128)} %copy.25.ids_ref, f32[128,2]{1,0:T(8,128)} %copy.26.weight_ref, bf16[128,192]{1,0:T(8,128)(2,1)} %copy.27.hidden_ref, bf16[3072,192]{1,0:T(8,128)(2,1)} %copy.28.wout_ref, bf16[2,6144,256]{2,1,0:T(8,128)(2,1)} %wg_hbm.1, ...), custom_call_target="tpu_custom_call" | custom-call | flops 10000000000 | bytes 20000000 | tf_op jit(solution)/shard_map/layer/pallas_call | solution.py:412
  110.7 1.6 %copy.29 = bf16[128,192]{0,1:T(8,128)(2,1)} copy(bf16[128,192]{1,0:T(8,128)(2,1)} %layer.1) | data formatting | bytes 98304 | tf_op jit(solution)/shard_map/layer/pallas_call | solution.py:412
  (1 shorter events, 0.0 us)
Async XLA Ops:
  0.0 7.5 %copy-start = (bf16[4,512,512]{2,1,0:T(8,128)(2,1)S(1)}, bf16[4,512,512]{2,1,0:T(8,128)(2,1)}, u32[]{:S(2)}) copy-start(bf16[4,512,512]{2,1,0:T(8,128)(2,1)} %param.16) | copy-start | bytes 6291460
  7.5 1.6 %copy-start.2 = (bf16[4,512,512]{2,1,0:T(8,128)(2,1)S(1)}, bf16[4,512,512]{2,1,0:T(8,128)(2,1)}, u32[]{:S(2)}) copy-start(bf16[4,512,512]{2,1,0:T(8,128)(2,1)} %param.17) | copy-start | bytes 6291460
  8.2 1.9 %copy-start.1 = (bf16[3072,192]{0,1:T(8,128)(2,1)S(1)}, bf16[3072,192]{0,1:T(8,128)(2,1)}, u32[]{:S(2)}) copy-start(bf16[3072,192]{0,1:T(8,128)(2,1)} %param.20) | copy-start | bytes 3538948

commit v2 on v0

v2 whole, which is shorter than its diff:
```python
import jax
import jax.numpy as jnp
from jax import lax
from jax.experimental import pallas as pl
from jax.experimental.pallas import tpu as pltpu
from jax.sharding import PartitionSpec as P

WIDTH = 6144
UNITS = 256
HEADS = 24
CONTEXT = 512

MESH = pl.DeviceIdType.MESH
floor_value = -1e30

GATHER_ORDER = ("zyx", "yxz", "xzy")
REDUCE_ORDER = ("xyz", "zxy", "yzx")
STEPS = (1, 3, 2)


def layer_kernel(
    len_ref, query_hbm, new_key_hbm, new_value_hbm, ids_hbm, weight_hbm, hidden_hbm,
    key_hbm, value_hbm, wout_hbm, wg_hbm, wu_hbm, wd_hbm,
    out_ref,
    query, new_key, new_value, ids, weight, hidden, keys, values, wout,
    wcat, wd, heads_in, heads_out, at, g, route, route_col, s, from_sib, ring1, ring2, ring3, acc, hs, mid, fin,
    lsem, ssem, rsem,
):
    f32, bf16 = jnp.float32, jnp.bfloat16
    pool, dev = lax.axis_index("pool"), lax.axis_index("dev")
    xl, c = pool // 2, pool % 2
    xh, y, z = dev // 16, (dev // 4) % 4, dev % 4
    x = 2 * xh + xl
    odd = (z % 2) == 1
    where_at = {"x": x, "y": y, "z": z}

    def ident(x_, y_, z_, c_):
        return ((x_ % 2) * 2 + c_, (x_ // 2) * 16 + y_ * 4 + z_)

    def near(**steps):
        p = {a: (where_at[a] + steps.get(a, 0)) % 4 for a in "xyz"}
        return ident(p["x"], p["y"], p["z"], c)

    sibling = ident(x, y, z, 1 - c)
    beside = x + 1 - 2 * xl
    beside_same = ident(beside, y, z, c)
    beside_other = ident(beside, y, z, 1 - c)

    barrier = pltpu.get_barrier_semaphore()
    greeted = [near(**{a: d}) for a in "xyz" for d in STEPS]
    greeted += [near(**{"x": 2, a: d}) for a in "yz" for d in STEPS]
    greeted += [sibling, beside_other]
    for who in greeted:
        pl.semaphore_signal(barrier, inc=1, device_id=who, device_id_type=MESH)

    local = []

    def fetch(src, dst):
        cp = pltpu.make_async_copy(src, dst, lsem.at[len(local)])
        cp.start()
        local.append(cp)

    for src, dst in ((query_hbm, query), (new_key_hbm, new_key), (new_value_hbm, new_value)):
        fetch(src, dst)
    for r in range(4):
        fetch(key_hbm.at[r], keys.at[r])
    for r in range(4):
        fetch(value_hbm.at[r], values.at[r])
    n_att = len(local)
    for src, dst in ((ids_hbm, ids), (weight_hbm, weight), (hidden_hbm, hidden), (wout_hbm, wout)):
        fetch(src, dst)
    n_mid = len(local)
    for e in range(2):
        for half in range(2):
            rows = pl.ds(half * (WIDTH // 2), WIDTH // 2)
            fetch(wg_hbm.at[e, rows], wcat.at[rows, pl.ds(e * 512, UNITS)])
            fetch(wu_hbm.at[e, rows], wcat.at[rows, pl.ds(e * 512 + UNITS, UNITS)])
    n_up = len(local)
    for e in range(2):
        fetch(wd_hbm.at[e], wd.at[pl.ds(e * UNITS, UNITS)])

    for cp in local[:3]:
        cp.wait()
    for h in range(HEADS):
        heads_in[h * 4:(h + 1) * 4, :] = query[:, h * 128:(h + 1) * 128].astype(f32)
    own = (lax.broadcasted_iota(jnp.int32, (HEADS, 512), 0) // 6) == (
        lax.broadcasted_iota(jnp.int32, (HEADS, 512), 1) // 128)
    position = lax.broadcasted_iota(jnp.int32, (HEADS, CONTEXT), 1)
    scale = 128 ** -0.5
    fresh_keys, fresh_values = new_key[...].astype(f32), new_value[...].astype(f32)
    spread, scores, fresh_scores, stats, sums = [], [], [], [], []
    for r in range(4):
        q1 = heads_in[pl.ds(r, HEADS, stride=4), :]
        spread.append(jnp.where(own, jnp.concatenate([q1] * 4, axis=1), 0.0))
        fresh_scores.append(jnp.sum(spread[r] * fresh_keys[r:r + 1, :], axis=1, keepdims=True) * scale)
    for r in range(4):
        local[3 + r].wait()
    for r in range(4):
        scores.append(lax.dot_general(
            spread[r].astype(bf16), keys[r], (((1,), (1,)), ((), ())), preferred_element_type=f32) * scale)
    for r in range(4):
        local[7 + r].wait()
    for r in range(4):
        usable = position < len_ref[r]
        row_max = jnp.max(jnp.where(usable, scores[r], floor_value), axis=1, keepdims=True)
        weights = jnp.where(usable, jnp.exp(scores[r] - row_max), 0.0)
        stats.append((row_max, jnp.sum(weights, axis=1, keepdims=True)))
        sums.append(jnp.dot(weights.astype(bf16), values[r], preferred_element_type=f32))
    for r in range(4):
        row_max, weight_total = stats[r]
        final_max = jnp.maximum(row_max, fresh_scores[r])
        cache_factor = jnp.exp(row_max - final_max)
        fresh_factor = jnp.exp(fresh_scores[r] - final_max)
        numerator = jnp.where(own, sums[r] * cache_factor + fresh_factor * fresh_values[r:r + 1, :], 0.0)
        numerator = (numerator[:, 0:128] + numerator[:, 128:256]) + (numerator[:, 256:384] + numerator[:, 384:512])
        heads_out[pl.ds(r, HEADS, stride=4), :] = numerator / (weight_total * cache_factor + fresh_factor)
    at[0, xh, y, z] = heads_out[0:48].astype(bf16)
    at[1, xh, y, z] = heads_out[48:96].astype(bf16)

    used = [0]
    sent = []

    def remote(src, dst, k, who):
        return pltpu.make_async_remote_copy(
            src_ref=src, dst_ref=dst, send_sem=ssem.at[k], recv_sem=rsem.at[k],
            device_id=who, device_id_type=MESH)

    def send(src, dst, who):
        k = used[0]
        used[0] += 1
        cp = remote(src, dst, k, who)
        cp.start()
        sent.append(cp)
        return cp

    pl.semaphore_wait(barrier, len(greeted))
    first, second = ("z", "y"), ("y", "z")
    arriving = []
    for q in range(2):
        block = at.at[q, xh, y, z]
        for dx in (0, 2):
            for d in (0, *STEPS):
                if dx or d:
                    arriving.append(send(block, block, near(**{"x": dx, first[q]: d})))

    for cp in local[n_att:n_mid]:
        cp.wait()
    expert = lax.broadcasted_iota(jnp.int32, (8, 128), 0)
    table = jnp.zeros((8, 128), f32)
    for k in range(2):
        table = table + jnp.where(ids[k:k + 1, :] == expert, weight[k:k + 1, :], 0.0)
    route[c, xl] = table
    route_copies = [send(route.at[c, xl], route.at[c, xl], who) for who in (sibling, beside_same, beside_other)]

    mid[:, 0:128] = hidden[0:128, :].astype(f32).T
    mid[:, 128:256] = jnp.concatenate([hidden[128:192, :].astype(f32), jnp.zeros((64, 128), f32)], axis=0).T

    for cp in arriving:
        cp.wait_recv()
    arriving = []
    for q in range(2):
        block = at.at[q, :, y] if q == 0 else at.at[q, :, :, z]
        arriving += [send(block, block, near(**{second[q]: d})) for d in STEPS]

    for cp in route_copies:
        cp.wait_recv()
    for e in range(2):
        for cc in range(2):
            for xi in range(2):
                row = jnp.sum(jnp.where(expert == 2 * pool + e, route[cc, xi], 0.0), axis=0, keepdims=True)
                col = jnp.broadcast_to(row, (128, 128)).T
                for t in range(2):
                    for half in range(2):
                        start = half * 128 + cc * 64 + xi * 32
                        route_col[e, t, start:start + 32, :] = col[t * 64 + half * 32:t * 64 + half * 32 + 32]

    for cp in arriving:
        cp.wait_recv()

    total = jnp.zeros((128, 192), f32)
    low = (lax.broadcasted_iota(jnp.int32, (16, 48, 128), 1) % 8) < 4
    for q in range(2):
        rows = at[q].astype(f32).reshape(16, 2, 48, 128)
        a, b = rows[:, 0], rows[:, 1]
        even = jnp.where(low, a, pltpu.roll(b, 4, 1)).reshape(16, 6, 8, 128)
        unev = jnp.where(low, pltpu.roll(a, 44, 1), b).reshape(16, 6, 8, 128)
        heads = []
        for v in range(6):
            heads.append(even[:, v].reshape(128, 128).astype(bf16))
            heads.append(unev[:, v].reshape(128, 128).astype(bf16))
        total = total + lax.dot_general(
            jnp.concatenate(heads, axis=1), wout[:, q * 1536:(q + 1) * 1536],
            (((1,), (1,)), ((), ())), preferred_element_type=f32)
    mid[:, 0:192] = (mid[:, 0:192] + total).astype(bf16).astype(f32)

    lane = lax.broadcasted_iota(jnp.int32, (128, 128), 1) < 64
    lane32 = lax.broadcasted_iota(jnp.int32, (32, 128), 1) < 64
    lane64 = lax.broadcasted_iota(jnp.int32, (64, 128), 1) < 64

    def view(ref, lead, order, stage, i, open_before):
        where = []
        for axis in "xyz":
            k = order.index(axis)
            is_open = k < stage if open_before else k > stage
            where.append(i if k == stage else slice(None) if is_open else where_at[axis])
        return ref.at[(*lead, *where)]

    def gather_view(t, q, stage, i):
        return view(g, (t, q, c), GATHER_ORDER[q], stage, i, True)

    last_at, pass_at, sib_at, sum_at = 60, 78, 102, 118

    def gather_copy(t, stage, q, n, k):
        axis, d = GATHER_ORDER[q][stage], STEPS[n]
        block = gather_view(t, q, stage, where_at[axis])
        return remote(block, block, k, near(**{axis: d}))

    def last_copy(t, q, n):
        return gather_copy(t, 2, q, n, last_at + t * 9 + q * 3 + n)

    def pass_copy(t, q, n):
        back = ((0, *STEPS)[n])
        block = gather_view(t, q, 2, (where_at[GATHER_ORDER[q][2]] + 4 - back) % 4)
        return remote(block, block, pass_at + t * 12 + q * 4 + n, sibling)

    def gather_start(t, stage):
        got = []
        for q in range(3):
            for n in range(3):
                axis = GATHER_ORDER[q][stage]
                block = gather_view(t, q, stage, where_at[axis])
                got.append(send(block, block, near(**{axis: STEPS[n]})))
        return got

    t0, t1 = mid[:, 0:128], mid[:, 128:256]
    whole = jnp.where(odd, jnp.where(lane, pltpu.roll(t0, 64, 1), pltpu.roll(t1, 64, 1)), t0)
    flight = []
    for t in range(2):
        a, b = t0[t * 64:(t + 1) * 64], t1[t * 64:(t + 1) * 64]
        packed = jnp.where(
            odd,
            jnp.where(lane32, a[32:64], pltpu.roll(a[0:32], 64, 1)),
            jnp.where(lane32, b[0:32], pltpu.roll(b[32:64], 64, 1)),
        )
        g[t, 0, c, x, y, z] = whole[t * 64:t * 64 + 32].astype(bf16)
        g[t, 1, c, x, y, z] = whole[t * 64 + 32:t * 64 + 64].astype(bf16)
        g[t, 2, c, x, y, z] = packed.astype(bf16)
        flight.append(gather_start(t, 0))
    for t in range(2):
        for cp in flight[t]:
            cp.wait_recv()
        flight[t] = gather_start(t, 1)
    for t in range(2):
        for cp in flight[t]:
            cp.wait_recv()
        for q in range(3):
            for n in range(3):
                last_copy(t, q, n).start()
        for q in range(3):
            pass_copy(t, q, 0).start()
    assert used[0] <= last_at

    def gather_end(t):
        for n in range(3):
            for q in range(3):
                last_copy(t, q, n).wait_recv()
                pass_copy(t, q, n + 1).start()

    def gate_and_up(t):
        acc[...] = jnp.zeros((256, 1024), f32)

        @pl.loop(0, 8, unroll=8)
        def _(i):
            xi, yi = i // 4, i % 4
            tiles = []
            for zp in range(2):
                pieces = []
                for zz in range(2):
                    pieces.append(g[t, 0:2, :, pl.ds(2 * xi, 2), yi, 2 * zp + zz].reshape(256, 128))
                h0 = g[t, 2, :, pl.ds(2 * xi, 2), yi, 2 * zp].astype(f32).reshape(128, 128)
                h1 = g[t, 2, :, pl.ds(2 * xi, 2), yi, 2 * zp + 1].astype(f32).reshape(128, 128)
                upper = jnp.where(lane, h0, h1)
                lower = pltpu.roll(jnp.where(lane, h1, h0), 64, 1)
                halves = jnp.concatenate([upper, lower], axis=0).astype(bf16)
                tiles += [pieces[0], halves, pieces[1]]
            lhs = jnp.concatenate(tiles, axis=1)
            rhs = wcat[pl.ds(pl.multiple_of(i * 768, 768), 768), :]
            acc[...] += jnp.dot(lhs, rhs, preferred_element_type=f32)

        for e in range(2):
            col = route_col[e, t]
            for k in range(2):
                gate = acc[:, e * 512 + k * 128:e * 512 + (k + 1) * 128]
                up = acc[:, e * 512 + 256 + k * 128:e * 512 + 256 + (k + 1) * 128]
                hs[:, e * 256 + k * 128:e * 256 + (k + 1) * 128] = (
                    gate / (1.0 + jnp.exp(-gate)) * up * col).astype(bf16)

    def sib_copy(t, i):
        part = (pl.ds(2 * (i // 4), 2), i % 4)
        return pltpu.make_async_remote_copy(
            src_ref=s.at[(t, slice(None), 1 - c, *part)], dst_ref=from_sib.at[(t, slice(None), *part)],
            send_sem=ssem.at[sib_at + 8 * t + i], recv_sem=rsem.at[sib_at + 8 * t + i],
            device_id=sibling, device_id_type=MESH)

    def down(t):
        @pl.loop(0, 8, unroll=8)
        def _(i):
            xi, yi = i // 4, i % 4
            out = jnp.dot(
                hs[...], wd[:, pl.ds(pl.multiple_of(i * 768, 768), 768)], preferred_element_type=f32)
            for zp in range(2):
                tiles = [out[:, zp * 384 + k * 128:zp * 384 + (k + 1) * 128] for k in range(3)]
                upper = tiles[1][0:128]
                lower = pltpu.roll(tiles[1][128:256], 64, 1)
                halves = (jnp.where(lane, upper, lower), jnp.where(lane, lower, upper))
                for zz in range(2):
                    there = (pl.ds(2 * xi, 2), yi, 2 * zp + zz)
                    s[(t, pl.ds(0, 2), slice(None), *there)] = tiles[2 * zz].astype(bf16).reshape(2, 2, 2, 32, 128)
                    s[(t, 2, slice(None), *there)] = halves[zz].astype(bf16).reshape(2, 2, 32, 128)
            sib_copy(t, i).start()

    def add_sibling(t):
        @pl.loop(0, 8, unroll=8)
        def _(i):
            part = (pl.ds(2 * (i // 4), 2), i % 4)
            sib_copy(t, i).wait_recv()
            mine = s[(t, slice(None), c, *part)].astype(f32)
            other = from_sib[(t, slice(None), *part)].astype(f32)
            s[(t, slice(None), c, *part)] = (mine + other).astype(bf16)

    rings = (ring1, ring2, ring3)

    def sum_view(t, q, stage, i):
        return view(s, (t, q, c), REDUCE_ORDER[q], stage, i, False)

    def sum_copy(t, stage, q, n):
        axis, d = REDUCE_ORDER[q][stage], STEPS[n]
        return remote(
            sum_view(t, q, stage, (where_at[axis] + d) % 4), rings[stage].at[t, q, n],
            sum_at + t * 27 + stage * 9 + q * 3 + n, near(**{axis: d}))

    def sum_start(t, stage):
        for q in range(3):
            for n in range(3):
                sum_copy(t, stage, q, n).start()

    def sum_end(t, stage):
        for q in range(3):
            for n in range(3):
                sum_copy(t, stage, q, n).wait_recv()
            v = sum_view(t, q, stage, where_at[REDUCE_ORDER[q][stage]])
            r = rings[stage]
            added = (v[...].astype(f32) + r[t, q, 0].astype(f32)) + (r[t, q, 1].astype(f32) + r[t, q, 2].astype(f32))
            if stage < 2:
                v[...] = added.astype(bf16)
            else:
                fin[t, q] = added

    for cp in local[n_mid:]:
        cp.wait()
    gather_end(0)

    @pl.loop(0, 2)
    def _(t):
        for q in range(3):
            for n in range(4):
                pass_copy(t, q, n).wait_recv()
        gate_and_up(t)

        @pl.when(t == 0)
        def _():
            gather_end(1)

        @pl.when(t == 1)
        def _():
            add_sibling(0)
            sum_start(0, 0)

        down(t)

    add_sibling(1)
    sum_start(1, 0)
    for stage in range(3):
        for t in range(2):
            sum_end(t, stage)
            if stage < 2:
                sum_start(t, stage + 1)

    for t in range(2):
        whole = fin[t, 0:2].reshape(64, 128)
        rolled = pltpu.roll(whole, 64, 1)
        f2 = fin[t, 2]
        r2 = pltpu.roll(f2, 64, 1)
        rows = slice(t * 64, (t + 1) * 64)
        mid[rows, 0:128] += jnp.where(
            odd, jnp.where(lane64, jnp.concatenate([r2, f2], axis=0), rolled), whole)
        mid[rows, 128:256] += jnp.where(odd, rolled, jnp.concatenate([f2, r2], axis=0))
    out_ref[0:128, :] = mid[:, 0:128].T.astype(bf16)
    out_ref[128:192, :] = mid[:, 128:256].T[0:64].astype(bf16)

    for cp in sent:
        cp.wait_send()
    for q in range(3):
        for n in range(3):
            last_copy(0, q, n).wait_send()
            last_copy(1, q, n).wait_send()

    @pl.loop(0, 2)
    def _(t):
        for q in range(3):
            for n in range(4):
                pass_copy(t, q, n).wait_send()
            for n in range(3):
                for stage in range(3):
                    sum_copy(t, stage, q, n).wait_send()

        @pl.loop(0, 8)
        def _(i):
            sib_copy(t, i).wait_send()


def shards(
    query,
    new_key,
    new_value,
    key_cache,
    value_cache,
    lengths,
    hidden_in,
    w_out,
    expert_ids,
    gate_weights,
    w_gate,
    w_up,
    w_down,
):
    bf16, f32 = jnp.bfloat16, jnp.float32
    hbm = pl.BlockSpec(memory_space=pl.ANY)
    mixed = pl.pallas_call(
        layer_kernel,
        out_shape=jax.ShapeDtypeStruct((192, 128), bf16),
        in_specs=[pl.BlockSpec(memory_space=pltpu.SMEM)] + [hbm] * 12,
        out_specs=pl.BlockSpec(memory_space=pltpu.VMEM),
        scratch_shapes=[
            pltpu.VMEM((4, 3072), bf16),
            pltpu.VMEM((4, 512), bf16),
            pltpu.VMEM((4, 512), bf16),
            pltpu.VMEM((2, 128), jnp.int32),
            pltpu.VMEM((2, 128), f32),
            pltpu.VMEM((192, 128), bf16),
            pltpu.VMEM((4, CONTEXT, 512), bf16),
            pltpu.VMEM((4, CONTEXT, 512), bf16),
            pltpu.VMEM((192, 3072), bf16),
            pltpu.VMEM((WIDTH, 4 * UNITS), bf16),
            pltpu.VMEM((2 * UNITS, WIDTH), bf16),
            pltpu.VMEM((96, 128), f32),
            pltpu.VMEM((96, 128), f32),
            pltpu.VMEM((2, 2, 4, 4, 48, 128), bf16),
            pltpu.VMEM((2, 3, 2, 4, 4, 4, 32, 128), bf16),
            pltpu.VMEM((2, 2, 8, 128), f32),
            pltpu.VMEM((2, 2, 256, 128), f32),
            pltpu.VMEM((2, 3, 2, 4, 4, 4, 32, 128), bf16),
            pltpu.VMEM((2, 3, 4, 4, 4, 32, 128), bf16),
            pltpu.VMEM((2, 3, 3, 4, 4, 32, 128), bf16),
            pltpu.VMEM((2, 3, 3, 4, 32, 128), bf16),
            pltpu.VMEM((2, 3, 3, 32, 128), bf16),
            pltpu.VMEM((256, 1024), f32),
            pltpu.VMEM((256, 512), bf16),
            pltpu.VMEM((128, 256), f32),
            pltpu.VMEM((2, 3, 32, 128), f32),
            pltpu.SemaphoreType.DMA((26,)),
            pltpu.SemaphoreType.DMA((172,)),
            pltpu.SemaphoreType.DMA((172,)),
        ],
        compiler_params=pltpu.CompilerParams(
            collective_id=0, has_side_effects=True, vmem_limit_bytes=60 * 1024 * 1024
        ),
        cost_estimate=pl.CostEstimate(flops=10_000_000_000, bytes_accessed=25_000_000, transcendentals=0),
        name="layer",
    )(
        lengths, query, new_key, new_value, expert_ids.T, gate_weights.T, hidden_in.T,
        key_cache, value_cache, w_out.T, w_gate, w_up, w_down,
    )
    return mixed.T


def solution(mesh):
    return jax.shard_map(
        shards,
        mesh=mesh,
        in_specs=(
            P(("pool", "dev"), None),
            P(("pool", "dev"), None),
            P(("pool", "dev"), None),
            P(("pool", "dev"), None, None),
            P(("pool", "dev"), None, None),
            P(("pool", "dev")),
            P("pool", "dev"),
            P(None, "dev"),
            P("pool", None),
            P("pool", None),
            P("pool", None, "dev"),
            P("pool", None, "dev"),
            P("pool", "dev", None),
        ),
        out_specs=P("pool", "dev"),
        check_vma=False,
    )
```

time: 629 us -> 79.3 us (0.13)
  waiting for transfers between devices: 334 us -> 0 us
  blocking collectives: 191 us -> 0 us
  Pallas kernels: 0 us -> 77.7 us
  local copies, waits for them, and re-layouts: 56.4 us -> 1.42 us
  matrix products: 27.4 us -> 0 us
  between operations: 13.6 us -> 0.01 us
    unnamed x3 -> x0, waiting for transfers between devices: 261 us -> none
    all_gather x1 -> x0, blocking collectives: 101 us -> none  [shards(): lax.all_gather(attended, 'dev', axis=0, tiled=True)]
    all_to_all x1 -> x0, blocking collectives: 90.2 us -> none  [shards(): lax.all_to_all(outgoing, 'pool', split_axis=0, concat_axis=0, tiled=True)]
    pallas_call x0 -> x1, Pallas kernels: none -> 77.7 us  [shards(): pl.pallas_call(layer_kernel, out_shape=jax.ShapeDtypeStruct((192, 128), b...]
    all_gather x1 -> x0, waiting for transfers between devices: 62.7 us -> none  [shards(): features = lax.all_gather(middle, 'dev', axis=1, tiled=True)]
    unnamed x23 -> x1, local copies, waits for them, and re-layouts: 52.7 us -> 1.42 us
    dot_general x9 -> x0, matrix products: 27.4 us -> none  [the longest x1 7.65 us: shards(): jnp.einsum('secf,efd->secd', hidden_units, w_down, preferred_element_type...]
    all_to_all x1 -> x0, waiting for transfers between devices: 10.2 us -> none  [shards(): lax.all_to_all(owned_sums, 'pool', split_axis=0, concat_axis=0, tiled=True)]
  transfers between devices with their start and end apart: 3 -> 0, of which waited for: 3 -> 0; matrix products, arithmetic and copies ran while one was open for 0% -> 0% of each run, Pallas kernels for 0% -> 0%
where the time goes in v2:
time: 79.3 us; the launch traced here: 79.2 us
  Pallas kernels  77.7 us (98%)
  local copies, waits for them, and re-layouts  1.42 us (2%)
    pallas_call x1, Pallas kernels, shards(): pl.pallas_call(layer_kernel, out_shape=jax.ShapeDtypeStruct((192, 128), b...  77.7 us

profile of v2, /device:TPU:0, one launch (start us, length us, event | category | flops | bytes accessed | tf_op | source)
XLA Modules:
  0.0 79.2 jit_solution(12963921068111077998)
XLA Ops:
  0.0 77.7 %layer.1 = bf16[192,128]{1,0:T(8,128)(2,1)} custom-call(s32[4]{0:T(128)} %len_ref.1, bf16[4,3072]{1,0:T(4,128)(2,1)} %query_hbm.1, bf16[4,512]{1,0:T(4,128)(2,1)} %new_key_hbm.1, bf16[4,512]{1,0:T(4,128)(2,1)} %new_value_hbm.1, s32[2,128]{1,0:T(2,128)} %bitcast.8, f32[2,128]{1,0:T(2,128)} %bitcast.9, bf16[192,128]{1,0:T(8,128)(2,1)} %bitcast.7, ...), custom_call_target="tpu_custom_call" | custom-call | flops 10000000000 | bytes 25000000 | tf_op jit(solution)/shard_map/layer/pallas_call | solution.py:439
  77.7 1.4 %copy.15 = bf16[128,192]{0,1:T(8,128)(2,1)} copy(bf16[128,192]{0,1:T(8,128)(2,1)} %bitcast.5) | data formatting | bytes 98304

commit v3 on v2

--- a/solution.py
+++ b/solution.py
@@ -23,7 +23,7 @@
     key_hbm, value_hbm, wout_hbm, wg_hbm, wu_hbm, wd_hbm,
     out_ref,
     query, new_key, new_value, ids, weight, hidden, keys, values, wout,
-    wcat, wd, heads_in, heads_out, at, g, route, route_col, s, from_sib, ring1, ring2, ring3, acc, hs, mid, fin,
+    wcat, wd, heads_in, heads_out, at, g, route, route_col, s, from_sib, ring1, ring2, ring3, acc, both, hs, mid, fin,
     lsem, ssem, rsem,
 ):
     f32, bf16 = jnp.float32, jnp.bfloat16
@@ -50,8 +50,6 @@
     greeted = [near(**{a: d}) for a in "xyz" for d in STEPS]
     greeted += [near(**{"x": 2, a: d}) for a in "yz" for d in STEPS]
     greeted += [sibling, beside_other]
-    for who in greeted:
-        pl.semaphore_signal(barrier, inc=1, device_id=who, device_id_type=MESH)
 
     local = []
 
@@ -66,6 +64,28 @@
         fetch(key_hbm.at[r], keys.at[r])
     for r in range(4):
         fetch(value_hbm.at[r], values.at[r])
+    for who in greeted:
+        pl.semaphore_signal(barrier, inc=1, device_id=who, device_id_type=MESH)
+
+    for cp in local[:3]:
+        cp.wait()
+    for h in range(HEADS):
+        heads_in[h * 4:(h + 1) * 4, :] = query[:, h * 128:(h + 1) * 128].astype(f32)
+    own = (lax.broadcasted_iota(jnp.int32, (HEADS, 512), 0) // 6) == (
+        lax.broadcasted_iota(jnp.int32, (HEADS, 512), 1) // 128)
+    position = lax.broadcasted_iota(jnp.int32, (HEADS, CONTEXT), 1)
+    scale = 128 ** -0.5
+    fresh_keys, fresh_values = new_key[...].astype(f32), new_value[...].astype(f32)
+    spread, scores, fresh_scores, stats, sums = [], [], [], [], []
+    for r in range(4):
+        q1 = heads_in[pl.ds(r, HEADS, stride=4), :]
+        spread.append(jnp.where(own, jnp.concatenate([q1] * 4, axis=1), 0.0))
+        fresh_scores.append(jnp.sum(spread[r] * fresh_keys[r:r + 1, :], axis=1, keepdims=True) * scale)
+    for r in range(4):
+        local[3 + r].wait()
+    for r in range(4):
+        scores.append(lax.dot_general(
+            spread[r].astype(bf16), keys[r], (((1,), (1,)), ((), ())), preferred_element_type=f32) * scale)
     n_att = len(local)
     for src, dst in ((ids_hbm, ids), (weight_hbm, weight), (hidden_hbm, hidden), (wout_hbm, wout)):
         fetch(src, dst)
@@ -78,26 +98,6 @@
     n_up = len(local)
     for e in range(2):
         fetch(wd_hbm.at[e], wd.at[pl.ds(e * UNITS, UNITS)])
-
-    for cp in local[:3]:
-        cp.wait()
-    for h in range(HEADS):
-        heads_in[h * 4:(h + 1) * 4, :] = query[:, h * 128:(h + 1) * 128].astype(f32)
-    own = (lax.broadcasted_iota(jnp.int32, (HEADS, 512), 0) // 6) == (
-        lax.broadcasted_iota(jnp.int32, (HEADS, 512), 1) // 128)
-    position = lax.broadcasted_iota(jnp.int32, (HEADS, CONTEXT), 1)
-    scale = 128 ** -0.5
-    fresh_keys, fresh_values = new_key[...].astype(f32), new_value[...].astype(f32)
-    spread, scores, fresh_scores, stats, sums = [], [], [], [], []
-    for r in range(4):
-        q1 = heads_in[pl.ds(r, HEADS, stride=4), :]
-        spread.append(jnp.where(own, jnp.concatenate([q1] * 4, axis=1), 0.0))
-        fresh_scores.append(jnp.sum(spread[r] * fresh_keys[r:r + 1, :], axis=1, keepdims=True) * scale)
-    for r in range(4):
-        local[3 + r].wait()
-    for r in range(4):
-        scores.append(lax.dot_general(
-            spread[r].astype(bf16), keys[r], (((1,), (1,)), ((), ())), preferred_element_type=f32) * scale)
     for r in range(4):
         local[7 + r].wait()
     for r in range(4):
@@ -197,18 +197,18 @@
     lane32 = lax.broadcasted_iota(jnp.int32, (32, 128), 1) < 64
     lane64 = lax.broadcasted_iota(jnp.int32, (64, 128), 1) < 64
 
-    def view(ref, lead, order, stage, i, open_before):
+    def view(ref, lead, order, stage, i, open_before, rows=slice(None)):
         where = []
         for axis in "xyz":
             k = order.index(axis)
             is_open = k < stage if open_before else k > stage
             where.append(i if k == stage else slice(None) if is_open else where_at[axis])
-        return ref.at[(*lead, *where)]
-
-    def gather_view(t, q, stage, i):
-        return view(g, (t, q, c), GATHER_ORDER[q], stage, i, True)
-
-    last_at, pass_at, sib_at, sum_at = 60, 78, 102, 118
+        return ref.at[(*lead, *where, rows)]
+
+    def gather_view(t, q, stage, i, rows=slice(None)):
+        return view(g, (t, q, c), GATHER_ORDER[q], stage, i, True, rows)
+
+    last_at, pass_at, sib_at, sum_at, half_at, far_at = 60, 78, 102, 118, 172, 184
 
     def gather_copy(t, stage, q, n, k):
         axis, d = GATHER_ORDER[q][stage], STEPS[n]
@@ -218,19 +218,20 @@
     def last_copy(t, q, n):
         return gather_copy(t, 2, q, n, last_at + t * 9 + q * 3 + n)
 
+    def far_copy(t, q, half):
+        axis, d = GATHER_ORDER[q][2], (1, 3)[half]
+        block = gather_view(t, q, 2, (where_at[axis] + 4 - d) % 4, pl.ds(half * 16, 16))
+        return remote(block, block, far_at + t * 3 + q if half else last_at + t * 9 + q * 3 + 2, near(**{axis: d}))
+
     def pass_copy(t, q, n):
         back = ((0, *STEPS)[n])
         block = gather_view(t, q, 2, (where_at[GATHER_ORDER[q][2]] + 4 - back) % 4)
         return remote(block, block, pass_at + t * 12 + q * 4 + n, sibling)
 
-    def gather_start(t, stage):
-        got = []
-        for q in range(3):
-            for n in range(3):
-                axis = GATHER_ORDER[q][stage]
-                block = gather_view(t, q, stage, where_at[axis])
-                got.append(send(block, block, near(**{axis: STEPS[n]})))
-        return got
+    def gather_start(t, stage, q):
+        axis = GATHER_ORDER[q][stage]
+        block = gather_view(t, q, stage, where_at[axis])
+        return [send(block, block, near(**{axis: d})) for d in STEPS]
 
     t0, t1 = mid[:, 0:128], mid[:, 128:256]
     whole = jnp.where(odd, jnp.where(lane, pltpu.roll(t0, 64, 1), pltpu.roll(t1, 64, 1)), t0)
@@ -245,26 +246,33 @@
         g[t, 0, c, x, y, z] = whole[t * 64:t * 64 + 32].astype(bf16)
         g[t, 1, c, x, y, z] = whole[t * 64 + 32:t * 64 + 64].astype(bf16)
         g[t, 2, c, x, y, z] = packed.astype(bf16)
-        flight.append(gather_start(t, 0))
+        flight.append([gather_start(t, 0, q) for q in range(3)])
     for t in range(2):
-        for cp in flight[t]:
-            cp.wait_recv()
-        flight[t] = gather_start(t, 1)
+        for q in range(3):
+            for cp in flight[t][q]:
+                cp.wait_recv()
+            flight[t][q] = gather_start(t, 1, q)
     for t in range(2):
-        for cp in flight[t]:
-            cp.wait_recv()
         for q in range(3):
-            for n in range(3):
+            for cp in flight[t][q]:
+                cp.wait_recv()
+            for n in range(2):
                 last_copy(t, q, n).start()
-        for q in range(3):
             pass_copy(t, q, 0).start()
     assert used[0] <= last_at
 
-    def gather_end(t):
-        for n in range(3):
+    def gather_on(t):
+        for n in range(2):
             for q in range(3):
                 last_copy(t, q, n).wait_recv()
+                far_copy(t, q, n).start()
                 pass_copy(t, q, n + 1).start()
+
+    def gather_end(t):
+        for q in range(3):
+            far_copy(t, q, 0).wait_recv()
+            far_copy(t, q, 1).wait_recv()
+            pass_copy(t, q, 3).start()
 
     def gate_and_up(t):
         acc[...] = jnp.zeros((256, 1024), f32)
@@ -303,13 +311,14 @@
             device_id=sibling, device_id_type=MESH)
 
     def down(t):
-        @pl.loop(0, 8, unroll=8)
-        def _(i):
+        def product(i):
+            both[i % 2] = jnp.dot(
+                hs[...], wd[:, pl.ds(pl.multiple_of(i * 768, 768), 768)], preferred_element_type=f32)
+
+        def place(i):
             xi, yi = i // 4, i % 4
-            out = jnp.dot(
-                hs[...], wd[:, pl.ds(pl.multiple_of(i * 768, 768), 768)], preferred_element_type=f32)
             for zp in range(2):
-                tiles = [out[:, zp * 384 + k * 128:zp * 384 + (k + 1) * 128] for k in range(3)]
+                tiles = [both[i % 2, :, zp * 384 + k * 128:zp * 384 + (k + 1) * 128] for k in range(3)]
                 upper = tiles[1][0:128]
                 lower = pltpu.roll(tiles[1][128:256], 64, 1)
                 halves = (jnp.where(lane, upper, lower), jnp.where(lane, lower, upper))
@@ -317,16 +326,24 @@
                     there = (pl.ds(2 * xi, 2), yi, 2 * zp + zz)
                     s[(t, pl.ds(0, 2), slice(None), *there)] = tiles[2 * zz].astype(bf16).reshape(2, 2, 2, 32, 128)
                     s[(t, 2, slice(None), *there)] = halves[zz].astype(bf16).reshape(2, 2, 32, 128)
-            sib_copy(t, i).start()
-
-    def add_sibling(t):
-        @pl.loop(0, 8, unroll=8)
+
+        product(0)
+
+        @pl.loop(1, 8)
         def _(i):
-            part = (pl.ds(2 * (i // 4), 2), i % 4)
-            sib_copy(t, i).wait_recv()
-            mine = s[(t, slice(None), c, *part)].astype(f32)
-            other = from_sib[(t, slice(None), *part)].astype(f32)
-            s[(t, slice(None), c, *part)] = (mine + other).astype(bf16)
+            place(i - 1)
+            product(i)
+            sib_copy(t, i - 1).start()
+
+        place(7)
+        sib_copy(t, 7).start()
+
+    def add_sibling(t, half):
+        @pl.loop(0, 4, unroll=2)
+        def _(yi):
+            part = (pl.ds(2 * half, 2), yi)
+            sib_copy(t, 4 * half + yi).wait_recv()
+            s[(t, slice(None), c, *part)] = s[(t, slice(None), c, *part)] + from_sib[(t, slice(None), *part)]
 
     rings = (ring1, ring2, ring3)
 
@@ -339,25 +356,49 @@
             sum_view(t, q, stage, (where_at[axis] + d) % 4), rings[stage].at[t, q, n],
             sum_at + t * 27 + stage * 9 + q * 3 + n, near(**{axis: d}))
 
-    def sum_start(t, stage):
-        for q in range(3):
+    def half_copy(t, q, n, half):
+        axis, d = REDUCE_ORDER[q][0], STEPS[n]
+        i = (where_at[axis] + d) % 4
+        xs = pl.ds(2 * half, 2)
+        src = s.at[t, q, c, xs, :, i] if axis == "z" else s.at[t, q, c, xs, i]
+        k = half_at + t * 6 + (q - 1) * 3 + n if half else sum_at + t * 27 + q * 3 + n
+        return remote(src, ring1.at[t, q, n, xs], k, near(**{axis: d}))
+
+    def first_sums(t):
+        for half in range(2):
+            add_sibling(t, half)
             for n in range(3):
-                sum_copy(t, stage, q, n).start()
-
-    def sum_end(t, stage):
-        for q in range(3):
-            for n in range(3):
+                @pl.when((x + STEPS[n]) % 4 // 2 == half)
+                def _():
+                    sum_copy(t, 0, 0, n).start()
+                for q in (1, 2):
+                    half_copy(t, q, n, half).start()
+
+    def sum_start(t, stage, q):
+        for n in range(3):
+            sum_copy(t, stage, q, n).start()
+
+    def sum_end(t, stage, q):
+        for n in range(3):
+            if stage == 0 and q > 0:
+                half_copy(t, q, n, 0).wait_recv()
+                half_copy(t, q, n, 1).wait_recv()
+            else:
                 sum_copy(t, stage, q, n).wait_recv()
-            v = sum_view(t, q, stage, where_at[REDUCE_ORDER[q][stage]])
-            r = rings[stage]
-            added = (v[...].astype(f32) + r[t, q, 0].astype(f32)) + (r[t, q, 1].astype(f32) + r[t, q, 2].astype(f32))
-            if stage < 2:
-                v[...] = added.astype(bf16)
-            else:
-                fin[t, q] = added
+        v = sum_view(t, q, stage, where_at[REDUCE_ORDER[q][stage]])
+        r = rings[stage]
+        added = (v[...].astype(f32) + r[t, q, 0].astype(f32)) + (r[t, q, 1].astype(f32) + r[t, q, 2].astype(f32))
+        if stage < 2:
+            v[...] = added.astype(bf16)
+            sum_start(t, stage + 1, q)
+        else:
+            fin[t, q] = added
 
     for cp in local[n_mid:]:
         cp.wait()
+
+    gather_on(0)
+    gather_on(1)
     gather_end(0)
 
     @pl.loop(0, 2)
@@ -365,6 +406,7 @@
         for q in range(3):
             for n in range(4):
                 pass_copy(t, q, n).wait_recv()
+
         gate_and_up(t)
 
         @pl.when(t == 0)
@@ -373,18 +415,47 @@
 
         @pl.when(t == 1)
         def _():
-            add_sibling(0)
-            sum_start(0, 0)
+            first_sums(0)
 
         down(t)
 
-    add_sibling(1)
-    sum_start(1, 0)
+    first_sums(1)
+
+    for cp in sent:
+        cp.wait_send()
+
+    @pl.loop(0, 2)
+    def _(t):
+        for q in range(3):
+            for n in range(2):
+                last_copy(t, q, n).wait_send()
+                far_copy(t, q, n).wait_send()
+            for n in range(4):
+                pass_copy(t, q, n).wait_send()
+
+        @pl.loop(0, 8)
+        def _(i):
+            sib_copy(t, i).wait_send()
+
+    def sums_left(stage):
+        @pl.loop(0, 2)
+        def _(t):
+            for q in range(3):
+                for n in range(3):
+                    if stage == 0 and q > 0:
+                        half_copy(t, q, n, 0).wait_send()
+                        half_copy(t, q, n, 1).wait_send()
+                    else:
+                        sum_copy(t, stage, q, n).wait_send()
+
     for stage in range(3):
-        for t in range(2):
-            sum_end(t, stage)
-            if stage < 2:
-                sum_start(t, stage + 1)
+        @pl.loop(0, 2)
+        def _(t):
+            for q in range(3):
+                sum_end(t, stage, q)
+
+        if stage < 2:
+            sums_left(stage)
 
     for t in range(2):
         whole = fin[t, 0:2].reshape(64, 128)
@@ -398,25 +469,7 @@
     out_ref[0:128, :] = mid[:, 0:128].T.astype(bf16)
     out_ref[128:192, :] = mid[:, 128:256].T[0:64].astype(bf16)
 
-    for cp in sent:
-        cp.wait_send()
-    for q in range(3):
-        for n in range(3):
-            last_copy(0, q, n).wait_send()
-            last_copy(1, q, n).wait_send()
-
-    @pl.loop(0, 2)
-    def _(t):
-        for q in range(3):
-            for n in range(4):
-                pass_copy(t, q, n).wait_send()
-            for n in range(3):
-                for stage in range(3):
-                    sum_copy(t, stage, q, n).wait_send()
-
-        @pl.loop(0, 8)
-        def _(i):
-            sib_copy(t, i).wait_send()
+    sums_left(2)
 
 
 def shards(
@@ -465,12 +518,13 @@
             pltpu.VMEM((2, 3, 3, 4, 32, 128), bf16),
             pltpu.VMEM((2, 3, 3, 32, 128), bf16),
             pltpu.VMEM((256, 1024), f32),
+            pltpu.VMEM((2, 256, 768), f32),
             pltpu.VMEM((256, 512), bf16),
             pltpu.VMEM((128, 256), f32),
             pltpu.VMEM((2, 3, 32, 128), f32),
             pltpu.SemaphoreType.DMA((26,)),
-            pltpu.SemaphoreType.DMA((172,)),
-            pltpu.SemaphoreType.DMA((172,)),
+            pltpu.SemaphoreType.DMA((190,)),
+            pltpu.SemaphoreType.DMA((190,)),
         ],
         compiler_params=pltpu.CompilerParams(
             collective_id=0, has_side_effects=True, vmem_limit_bytes=60 * 1024 * 1024

time: 79.3 us -> 78.9 us (level)
  Pallas kernels: 77.7 us -> 76.8 us
    pallas_call x1, Pallas kernels: 77.7 us -> 76.8 us  [shards(): pl.pallas_call(layer_kernel, out_shape=jax.ShapeDtypeStruct((192, 128), b...]
where the time goes in v3:
time: 78.9 us; the launch traced here: 78.2 us
  Pallas kernels  76.8 us (97%)
  local copies, waits for them, and re-layouts  1.42 us (2%)
    pallas_call x1, Pallas kernels, shards(): pl.pallas_call(layer_kernel, out_shape=jax.ShapeDtypeStruct((192, 128), b...  76.8 us

profile of v3, /device:TPU:0, one launch (start us, length us, event | category | flops | bytes accessed | tf_op | source)
XLA Modules:
  0.0 78.2 jit_solution(941804833967769729)
XLA Ops:
  0.0 76.8 %layer.1 = bf16[192,128]{1,0:T(8,128)(2,1)} custom-call(s32[4]{0:T(128)} %len_ref.1, bf16[4,3072]{1,0:T(4,128)(2,1)} %query_hbm.1, bf16[4,512]{1,0:T(4,128)(2,1)} %new_key_hbm.1, bf16[4,512]{1,0:T(4,128)(2,1)} %new_value_hbm.1, s32[2,128]{1,0:T(2,128)} %bitcast.8, f32[2,128]{1,0:T(2,128)} %bitcast.9, bf16[192,128]{1,0:T(8,128)(2,1)} %bitcast.7, ...), custom_call_target="tpu_custom_call" | custom-call | flops 10000000000 | bytes 25000000 | tf_op jit(solution)/shard_map/layer/pallas_call | solution.py:492
  76.8 1.4 %copy.15 = bf16[128,192]{0,1:T(8,128)(2,1)} copy(bf16[128,192]{0,1:T(8,128)(2,1)} %bitcast.5) | data formatting | bytes 98304

commit v4 on v3

--- a/solution.py
+++ b/solution.py
@@ -135,13 +135,13 @@
 
     pl.semaphore_wait(barrier, len(greeted))
     first, second = ("z", "y"), ("y", "z")
-    arriving = []
+    arriving = [[], []]
     for q in range(2):
         block = at.at[q, xh, y, z]
         for dx in (0, 2):
             for d in (0, *STEPS):
                 if dx or d:
-                    arriving.append(send(block, block, near(**{"x": dx, first[q]: d})))
+                    arriving[q].append(send(block, block, near(**{"x": dx, first[q]: d})))
 
     for cp in local[n_att:n_mid]:
         cp.wait()
@@ -155,12 +155,11 @@
     mid[:, 0:128] = hidden[0:128, :].astype(f32).T
     mid[:, 128:256] = jnp.concatenate([hidden[128:192, :].astype(f32), jnp.zeros((64, 128), f32)], axis=0).T
 
-    for cp in arriving:
-        cp.wait_recv()
-    arriving = []
     for q in range(2):
+        for cp in arriving[q]:
+            cp.wait_recv()
         block = at.at[q, :, y] if q == 0 else at.at[q, :, :, z]
-        arriving += [send(block, block, near(**{second[q]: d})) for d in STEPS]
+        arriving[q] = [send(block, block, near(**{second[q]: d})) for d in STEPS]
 
     for cp in route_copies:
         cp.wait_recv()
@@ -174,12 +173,11 @@
                         start = half * 128 + cc * 64 + xi * 32
                         route_col[e, t, start:start + 32, :] = col[t * 64 + half * 32:t * 64 + half * 32 + 32]
 
-    for cp in arriving:
-        cp.wait_recv()
-
     total = jnp.zeros((128, 192), f32)
     low = (lax.broadcasted_iota(jnp.int32, (16, 48, 128), 1) % 8) < 4
     for q in range(2):
+        for cp in arriving[q]:
+            cp.wait_recv()
         rows = at[q].astype(f32).reshape(16, 2, 48, 128)
         a, b = rows[:, 0], rows[:, 1]
         even = jnp.where(low, a, pltpu.roll(b, 4, 1)).reshape(16, 6, 8, 128)

time: 78.9 us -> 79 us (level)
  no operation moved by 1% of the time
where the time goes in v4:
time: 79 us; the launch traced here: 78.1 us
  Pallas kernels  76.6 us (97%)
  local copies, waits for them, and re-layouts  1.42 us (2%)
    pallas_call x1, Pallas kernels, shards(): pl.pallas_call(layer_kernel, out_shape=jax.ShapeDtypeStruct((192, 128), b...  76.6 us

profile of v4, /device:TPU:0, one launch (start us, length us, event | category | flops | bytes accessed | tf_op | source)
XLA Modules:
  0.0 78.1 jit_solution(13572947744589724849)
XLA Ops:
  0.0 76.6 %layer.1 = bf16[192,128]{1,0:T(8,128)(2,1)} custom-call(s32[4]{0:T(128)} %len_ref.1, bf16[4,3072]{1,0:T(4,128)(2,1)} %query_hbm.1, bf16[4,512]{1,0:T(4,128)(2,1)} %new_key_hbm.1, bf16[4,512]{1,0:T(4,128)(2,1)} %new_value_hbm.1, s32[2,128]{1,0:T(2,128)} %bitcast.8, f32[2,128]{1,0:T(2,128)} %bitcast.9, bf16[192,128]{1,0:T(8,128)(2,1)} %bitcast.7, ...), custom_call_target="tpu_custom_call" | custom-call | flops 10000000000 | bytes 25000000 | tf_op jit(solution)/shard_map/layer/pallas_call | solution.py:490
  76.6 1.4 %copy.15 = bf16[128,192]{0,1:T(8,128)(2,1)} copy(bf16[128,192]{0,1:T(8,128)(2,1)} %bitcast.5) | data formatting | bytes 98304
